TPU v7x, 128 devices: a whole 4x4x4 slice. The times are simulated.
128 devices in a mesh: row: 16 (over z_hi, x, core), col: 8 (over z_lo, y).
Axes of the slice: x: 4, y: 4, z: 4 (z_hi: 2, z_lo: 2; z = z_hi * 2 + z_lo), core: 2. Of those that a mesh axis runs over, the one named last changes fastest.
Arguments:
- queries: bfloat16 [16384, 512], P(('row', 'col'))
- keys: bfloat16 [16384, 128], P(('row', 'col'))
- values: bfloat16 [16384, 128], P(('row', 'col')), may hold values from -6 to 6
- outputs: bfloat16 [16384, 512], P(('row', 'col')), may hold values from -6 to 6
- grad_out: bfloat16 [16384, 512], P(('row', 'col')), may hold values from -6 to 6
- block_order: int32 [128], replicated, may hold values from 0 to 127, each once
Outputs:
- grad_queries: bfloat16 [16384, 512], P(('row', 'col'))
- grad_keys: bfloat16 [16384, 128], P(('row', 'col'))
- grad_values: bfloat16 [16384, 128], P(('row', 'col'))
Inputs may be any that keep to these rules, and one draw needn't show every extreme that they name: `block_order`: each slot holds a different block.
All inputs are finite; a program needn't handle non-finite values.
Results may differ from a plain program's by a relative error of at most 0.017.
Values may be sent and summed in bfloat16 or wider, within the bound.
A program may use at most 128 MiB of HBM per device.

v0:
```python
import math

import jax
import jax.numpy as jnp
from jax import lax
from jax.sharding import PartitionSpec as P


def joined(shard, axis, combine):
    everything = jax.tree.map(lambda part: lax.all_gather(part, axis), shard)
    first = jax.tree.map(lambda part: part[0], everything)

    def hop(k, so_far):
        return combine(so_far, jax.tree.map(lambda part: part[k], everything))

    return lax.fori_loop(1, lax.axis_size(axis), hop, first)


def combine_stats(first, second):
    top = jnp.maximum(first[0], second[0])
    return (top, first[1] * jnp.exp(first[0] - top) + second[1] * jnp.exp(second[0] - top))


def head_delta(cotangent, forward, head_count, head_size):
    product = cotangent.astype(jnp.float32) * forward.astype(jnp.float32)
    return jnp.sum(product.reshape(product.shape[0], head_count, head_size), axis=-1)


def tile_scores(query_all, key_all, causal, number, head_size, factor):
    query_head = query_all[:, number * head_size : (number + 1) * head_size]
    raw = lax.dot_general(
        query_head, key_all, (((1,), (1,)), ((), ())), preferred_element_type=jnp.float32
    )
    return jnp.where(causal, raw * factor, -1e30)


def local_stats(query_all, key_all, causal, head_count, head_size, factor):
    largest_list = []
    total_list = []
    for number in range(head_count):
        scores = tile_scores(query_all, key_all, causal, number, head_size, factor)
        largest = jnp.max(scores, axis=1)
        total = jnp.sum(jnp.where(causal, jnp.exp(scores - largest[:, None]), 0.0), axis=1)
        largest_list.append(largest)
        total_list.append(total)
    return (jnp.stack(largest_list, axis=1), jnp.stack(total_list, axis=1))


def tile_grads(
    query_all, cot_all, delta, key_all, value_all, causal, log_total, head_count, head_size, factor
):
    grad_k = jnp.zeros(key_all.shape, jnp.float32)
    grad_v = jnp.zeros(value_all.shape, jnp.float32)
    grad_parts = []
    for number in range(head_count):
        scores = tile_scores(query_all, key_all, causal, number, head_size, factor)
        probs = jnp.where(causal, jnp.exp(scores - log_total[:, number][:, None]), 0.0)
        probs_half = probs.astype(jnp.bfloat16)
        cot_head = cot_all[:, number * head_size : (number + 1) * head_size]
        query_head = query_all[:, number * head_size : (number + 1) * head_size]
        grad_p = lax.dot_general(
            cot_head, value_all, (((1,), (1,)), ((), ())), preferred_element_type=jnp.float32
        )
        grad_s = (probs * (grad_p - delta[:, number][:, None]) * factor).astype(jnp.bfloat16)
        grad_parts.append(jnp.dot(grad_s, key_all, preferred_element_type=jnp.float32))
        grad_k = grad_k + lax.dot_general(
            grad_s, query_head, (((0,), (0,)), ((), ())), preferred_element_type=jnp.float32
        )
        grad_v = grad_v + lax.dot_general(
            probs_half, cot_head, (((0,), (0,)), ((), ())), preferred_element_type=jnp.float32
        )
    return (jnp.concatenate(grad_parts, axis=1), grad_k, grad_v)


def visibility(block_order, query_slots, key_slots, block_rows):
    within = jnp.arange(block_rows, dtype=jnp.int32)
    query_pos = (block_order[query_slots][:, None] * block_rows + within[None, :]).reshape(-1)
    key_pos = (block_order[key_slots][:, None] * block_rows + within[None, :]).reshape(-1)
    return key_pos[None, :] <= query_pos[:, None]


def per_device(queries, keys, values, outputs, grad_out, block_order):
    row_count = lax.axis_size("row")
    col_count = lax.axis_size("col")
    row_index = lax.axis_index("row")
    col_index = lax.axis_index("col")
    block_rows = queries.shape[0]
    head_size = keys.shape[1]
    head_count = queries.shape[1] // head_size
    factor = 1.0 / math.sqrt(head_size)
    local_delta = head_delta(grad_out, outputs, head_count, head_size)
    query_all, cot_all = (
        lax.all_gather(queries, "row", axis=0, tiled=True),
        lax.all_gather(grad_out, "row", axis=0, tiled=True),
    )
    delta = lax.all_gather(local_delta, "row", axis=0, tiled=True)
    key_all, value_all = (
        lax.all_gather(keys, "col", axis=0, tiled=True),
        lax.all_gather(values, "col", axis=0, tiled=True),
    )
    query_slots = jnp.arange(row_count, dtype=jnp.int32) * col_count + col_index
    key_slots = row_index * col_count + jnp.arange(col_count, dtype=jnp.int32)
    causal = visibility(block_order, query_slots, key_slots, block_rows)
    largest, total = local_stats(query_all, key_all, causal, head_count, head_size, factor)
    largest, total = joined((largest, total), "row", combine_stats)
    log_total = largest + jnp.log(total)
    grad_q, grad_k, grad_v = tile_grads(
        query_all,
        cot_all,
        delta,
        key_all,
        value_all,
        causal,
        log_total,
        head_count,
        head_size,
        factor,
    )
    grad_q = lax.psum_scatter(
        grad_q.astype(jnp.bfloat16), "row", scatter_dimension=0, tiled=True
    ).astype(jnp.float32)
    grad_k, grad_v = (
        lax.psum_scatter(
            grad_k.astype(jnp.bfloat16), "col", scatter_dimension=0, tiled=True
        ).astype(jnp.float32),
        lax.psum_scatter(
            grad_v.astype(jnp.bfloat16), "col", scatter_dimension=0, tiled=True
        ).astype(jnp.float32),
    )
    return (grad_q.astype(jnp.bfloat16), grad_k.astype(jnp.bfloat16), grad_v.astype(jnp.bfloat16))


def solution(mesh):
    placed = (
        P(("row", "col"), None),
        P(("row", "col"), None),
        P(("row", "col"), None),
        P(("row", "col"), None),
        P(("row", "col"), None),
        P(),
    )
    return jax.shard_map(
        per_device,
        mesh=mesh,
        in_specs=placed,
        out_specs=(P(("row", "col"), None), P(("row", "col"), None), P(("row", "col"), None)),
        check_vma=False,
    )
```

profile of v0, /device:TPU:1, one launch (start us, length us, event | category | flops | bytes accessed | tf_op | source)
XLA Modules:
  0.0 333.3 jit_solution(1431649139815027245)
XLA Ops:
  7.2 0.7 all-gather.5.cloned.1.call-update
  8.0 0.7 all-gather.7.cloned.1.call-update
  8.8 0.7 gather_fusion.1
  9.4 0.1 add_bitcast_fusion
  9.5 0.6 gather_fusion
  10.2 0.1 add_bitcast_fusion.1
  10.2 24.6 %all_gather.28 = bf16[1024,128]{1,0:T(8,128)(2,1)S(1)} all-gather(bf16[128,128]{1,0:T(8,128)(2,1)} %param.9), channel_id=1, replica_groups=mesh['row'=16,'col'=8] {'col'}, dimensions={0}, use_global_device_ids=true | all-gather | bytes 294912 | tf_op jit(solution)/shard_map/all_gather | solution.py:98
  34.8 1.0 convert_multiply_fusion
  35.8 0.1 reshape.84
  35.9 0.2 reduce_sum.49
  36.1 35.6 %all_gather.35 = f32[2048,4]{1,0:T(8,128)S(1)} all-gather(f32[128,4]{1,0:T(8,128)S(1)} %reduce_sum.49), channel_id=1, replica_groups=mesh['row'=16,'col'=8] {'row'}, dimensions={0}, use_global_device_ids=true | all-gather | bytes 34816 | tf_op jit(solution)/shard_map/all_gather | solution.py:96
  71.7 2.0 slice_reduce_fusion.3
  73.7 24.2 %all_gather.34 = bf16[1024,128]{1,0:T(8,128)(2,1)} all-gather(bf16[128,128]{1,0:T(8,128)(2,1)S(1)} %copy-done.8), channel_id=1, replica_groups=mesh['row'=16,'col'=8] {'col'}, dimensions={0}, use_global_device_ids=true | all-gather | bytes 294912 | tf_op jit(solution)/shard_map/all_gather | solution.py:99
  97.9 2.5 fusion.60
  100.4 1.3 fusion.61
  101.8 4.5 %fusion.62 = (f32[2048]{0:T(1024)S(1)}, f32[2048,1024]{0,1:T(8,128)}) fusion(bf16[1024,128]{1,0:T(8,128)(2,1)S(1)} %all_gather.28, bf16[2048,512]{1,0:T(8,128)(2,1)S(1)} %copy-done.6, s32[2048]{0:T(1024)S(1)} %add_bitcast_fusion, s32[1024]{0:T(1024)S(1)} %add_bitcast_fusion.1), kind=kOutput, calls=%fused_computation.95 | convolution fusion | flops 545257472 | bytes 9195520 | tf_op jit(solution)/shard_map/dot_general | solution.py:31
  106.3 1.3 fusion.59
  107.6 1.1 copy-done.4
  108.7 10.3 %fusion.2 = (f32[2048]{0:T(1024)S(1)}, f32[2048]{0:T(1024)S(1)}, f32[2048]{0:T(1024)S(1)}, f32[2048]{0:T(1024)S(1)}) fusion(f32[2048,1024]{0,1:T(8,128)} %get-tuple-element.178, f32[2048]{0:T(1024)S(1)} %get-tuple-element.177, s32[2048]{0:T(1024)S(1)} %add_bitcast_fusion, s32[1024]{0:T(1024)S(1)} %add_bitcast_fusion.1, ...), kind=kLoop, calls=%fused_computation.19 | loop fusion | flops 27254784 | bytes 33632256 | tf_op jit(solution)/shard_map/reduce_sum | solution.py:43
  119.1 27.0 %all-gather.1 = f32[32768,4]{0,1:T(4,128)S(1)} all-gather(f32[2048,4]{0,1:T(4,128)S(1)} %pad_maximum_fusion.2), channel_id=3, replica_groups=mesh['row'=16,'col'=8] {'row'}, dimensions={0}, use_global_device_ids=true | all-gather | bytes 557056 | tf_op jit(solution)/shard_map/all_gather | solution.py:10
  146.2 22.4 %all-gather = f32[32768,4]{0,1:T(4,128)S(1)} all-gather(f32[2048,4]{0,1:T(4,128)S(1)} %pad_maximum_fusion.1), channel_id=2, replica_groups=mesh['row'=16,'col'=8] {'row'}, dimensions={0}, use_global_device_ids=true | all-gather | bytes 557056 | tf_op jit(solution)/shard_map/all_gather | solution.py:10
  168.6 1.0 while.17
  168.7 0.1 fusion.84
  168.7 0.1 fusion.84
  169.8 4.7 %fusion.12 = f32[1024,128]{1,0:T(8,128)S(1)} fusion(f32[2048,1024]{0,1:T(8,128)} %copy-done.2, f32[2048]{0:T(1024)S(1)} %bitcast.77, s32[2048]{0:T(1024)S(1)} %add_bitcast_fusion, s32[1024]{0:T(1024)S(1)} %add_bitcast_fusion.1, bf16[2048,512]{1,0:T(8,128)(2,1)} %all-gather.7.cloned.1.call-done), kind=kOutput, calls=%fused_computation.32 | convolution fusion | flops 545259520 | bytes 9457664 | tf_op jit(solution)/shard_map/dot_general | solution.py:69
  174.4 1.3 copy-done.5
  175.7 0.6 copy-done.9
  176.3 1.5 fusion.14
  177.8 1.1 slice-done.3
  179.0 1.5 fusion.10
  180.5 0.9 slice-done.7
  181.4 2.4 fusion.32
  183.9 5.2 %multiply_convert_fusion.3 = bf16[2048,1024]{0,1:T(8,128)(2,1)S(1)} fusion(f32[2048,1024]{0,1:T(8,128)} %get-tuple-element.178, bf16[1024,128]{1,0:T(8,128)(2,1)S(1)} %copy-done.7, f32[2048]{0:T(1024)S(1)} %get-tuple-element.147, f32[2048]{0:T(1024)S(1)} %bitcast.82, s32[2048]{0:T(1024)S(1)} %add_bitcast_fusion, s32[1024]{0:T(1024)S(1)} %add_bitcast_fusion.1, ...), kind=kOutput, calls=%fused_computation.26 | convolution fusion | flops 551550976 | bytes 13398016 | tf_op jit(solution)/shard_map/dot_general | solution.py:61
  189.2 1.6 convolution_convert_fusion.3
  190.8 5.0 %multiply_convert_fusion.2 = bf16[2048,1024]{0,1:T(8,128)(2,1)S(1)} fusion(f32[2048,1024]{0,1:T(8,128)} %copy-done.4, bf16[1024,128]{1,0:T(8,128)(2,1)S(1)} %copy-done.7, f32[2048]{0:T(1024)S(1)} %get-tuple-element.150, f32[2048]{0:T(1024)S(1)} %bitcast.80, s32[2048]{0:T(1024)S(1)} %add_bitcast_fusion, s32[1024]{0:T(1024)S(1)} %add_bitcast_fusion.1, ...), kind=kOutput, calls=%fused_computation.25 | convolution fusion | flops 551550976 | bytes 13398016 | tf_op jit(solution)/shard_map/dot_general | solution.py:61
  195.8 1.6 convolution_convert_fusion.2
  197.4 1.2 fusion.49
  198.7 1.3 convolution_add_fusion.2
  200.0 2.9 multiply_convert_fusion.1
  202.9 3.1 multiply_convert_fusion
  206.1 1.3 convolution_add_fusion.1
  207.4 1.6 convolution_convert_fusion.1
  209.0 2.0 fusion.31
  211.1 3.0 convolution_convert_fusion
  214.0 1.6 pad_maximum_fusion
  215.6 2.5 copy.28
  218.2 31.0 %reduce-scatter.6.cloned.1.call-done = bf16[128,128]{1,0:T(8,128)(2,1)} async-done(((bf16[1024,128]{1,0:T(8,128)(2,1)}), bf16[128,128]{1,0:T(8,128)(2,1)}) %reduce-scatter.6.cloned.1.call-update) | async-done | bytes 32784 | tf_op jit(solution)/shard_map/reduce_scatter | solution.py:123
  249.1 77.7 %reduce-scatter.10.cloned.1.call-done = bf16[128,512]{1,0:T(8,128)(2,1)} async-done(((bf16[2048,512]{1,0:T(8,128)(2,1)}), bf16[128,512]{1,0:T(8,128)(2,1)}) %reduce-scatter.10.cloned.1.call-update) | async-done | bytes 131088
  (75 shorter events, 1.3 us)
Async XLA Ops:
  7.2 1.6 copy-start
  7.2 66.5 %copy-start.8 = (bf16[128,128]{1,0:T(8,128)(2,1)S(1)}, bf16[128,128]{1,0:T(8,128)(2,1)}, u32[]{:S(2)}) copy-start(bf16[128,128]{1,0:T(8,128)(2,1)} %param.10) | copy-start | bytes 98308
  7.2 90.7 %all-gather.5.cloned.1.call-start = ((), (), s32[]{:S(2)}) async-start(), calls=%async_computation.3 | async-start | bytes 2228224 | tf_op jit(solution)/shard_map/all_gather | solution.py:93
  7.9 161.8 %all-gather.7.cloned.1.call-start = ((), (), s32[]{:S(2)}) async-start(), calls=%async_computation.4 | async-start | bytes 2228224 | tf_op jit(solution)/shard_map/all_gather | solution.py:94
  8.7 209.5 %reduce-scatter.8.cloned.1.call-start = ((), (), s32[]{:S(2)}) async-start(), calls=%async_computation.6 | async-start | bytes 294912 | tf_op jit(solution)/shard_map/reduce_scatter | solution.py:126
  97.9 2.5 copy-start.6
  100.4 7.2 %copy-start.2 = (f32[2048,1024]{0,1:T(8,128)}, f32[2048,1024]{0,1:T(8,128)S(1)}, u32[]{:S(2)}) copy-start(f32[2048,1024]{0,1:T(8,128)S(1)} %get-tuple-element.174) | copy-start | bytes 25165828
  101.7 7.0 %copy-start.4 = (f32[2048,1024]{0,1:T(8,128)}, f32[2048,1024]{0,1:T(8,128)S(1)}, u32[]{:S(2)}) copy-start(f32[2048,1024]{0,1:T(8,128)S(1)} %get-tuple-element.176) | copy-start | bytes 25165828
  107.6 11.5 %copy-start.3 = (f32[2048,1024]{0,1:T(8,128)}, f32[2048,1024]{0,1:T(8,128)S(1)}, u32[]{:S(2)}) copy-start(f32[2048,1024]{0,1:T(8,128)S(1)} %get-tuple-element.172) | copy-start | bytes 25165828
  169.7 6.0 %copy-start.5 = (f32[2048,1024]{0,1:T(8,128)S(1)}, f32[2048,1024]{0,1:T(8,128)}, u32[]{:S(2)}) copy-start(f32[2048,1024]{0,1:T(8,128)} %copy-done.4) | copy-start | bytes 25165828
  169.7 6.6 %copy-start.9 = (bf16[2048,512]{1,0:T(8,128)(2,1)S(1)}, bf16[2048,512]{1,0:T(8,128)(2,1)}, u32[]{:S(2)}) copy-start(bf16[2048,512]{1,0:T(8,128)(2,1)} %all-gather.7.cloned.1.call-done) | copy-start | bytes 6291460
  169.7 8.1 %slice-start.2 = ((s8[8388608]{0:T(1024)(128)(4,1)}), s8[4194304]{0:T(1024)(128)(4,1)S(1)}, s32[]{:S(2)}) async-start(s8[8388608]{0:T(1024)(128)(4,1)} %bitcast.59), calls=%async_computation.10 | async-start | bytes 8388608
  176.3 2.6 slice-start.3
  176.3 4.1 %slice-start.6 = ((s8[8388608]{0:T(1024)(128)(4,1)}), s8[4194304]{0:T(1024)(128)(4,1)S(1)}, s32[]{:S(2)}) async-start(s8[8388608]{0:T(1024)(128)(4,1)} %bitcast.63), calls=%async_computation.14 | async-start | bytes 8388608
  179.0 2.4 slice-start.7
  180.4 3.4 %copy-start.7 = (bf16[1024,128]{1,0:T(8,128)(2,1)S(1)}, bf16[1024,128]{1,0:T(8,128)(2,1)}, u32[]{:S(2)}) copy-start(bf16[1024,128]{1,0:T(8,128)(2,1)} %all_gather.34) | copy-start | bytes 786436
  183.8 65.3 %reduce-scatter.6.cloned.1.call-start = ((), (), s32[]{:S(2)}) async-start(), calls=%async_computation.5 | async-start | bytes 294912 | tf_op jit(solution)/shard_map/reduce_scatter | solution.py:123
  183.9 6.9 %copy-start.10 = (bf16[2048,512]{1,0:T(8,128)(2,1)S(1)}, bf16[2048,512]{1,0:T(8,128)(2,1)}, u32[]{:S(2)}) copy-start(bf16[2048,512]{1,0:T(8,128)(2,1)} %all-gather.7.cloned.1.call-done) | copy-start | bytes 6291460
  195.8 4.1 %slice-start = ((s8[8388608]{0:T(1024)(128)(4,1)}), s8[4194304]{0:T(1024)(128)(4,1)S(1)}, s32[]{:S(2)}) async-start(s8[8388608]{0:T(1024)(128)(4,1)} %bitcast.57), calls=%async_computation.8 | async-start | bytes 8388608
  197.4 2.6 slice-start.1
  198.6 4.3 %slice-start.4 = ((s8[8388608]{0:T(1024)(128)(4,1)}), s8[4194304]{0:T(1024)(128)(4,1)S(1)}, s32[]{:S(2)}) async-start(s8[8388608]{0:T(1024)(128)(4,1)} %bitcast.61), calls=%async_computation.12 | async-start | bytes 8388608
  200.0 3.0 slice-start.5
  206.1 2.9 copy-start.11
  209.0 117.8 %copy-start.1 = (s32[128]{0:T(128)S(1)}, s32[128]{0:T(128)}, u32[]{:S(2)}) copy-start(s32[128]{0:T(128)} %param.13) | copy-start | bytes 1540
  211.0 115.8 %reduce-scatter.10.cloned.1.call-start = ((), (), s32[]{:S(2)}) async-start(), calls=%async_computation.7 | async-start | bytes 2228224
Sparse Core Ops, SparseCore 0:
  10.5 52.6 all-gather.4
  65.6 49.2 all-gather.6
  184.0 26.2 reduce-scatter.7
  213.1 35.9 reduce-scatter.5
  253.5 73.2 reduce-scatter.9
where the time goes:
time: 335 us; the launch traced here: 333 us
  blocking collectives  134 us (40%)
  waiting for transfers between devices  110 us (33%)
  matrix products  49.6 us (15%)
  other arithmetic  14.2 us (4%)
  between operations  14.2 us (4%)
  local copies, waits for them, and re-layouts  11.1 us (3%)
    unnamed x6, waiting for transfers between devices  79.1 us
    all_gather x2, blocking collectives, joined(): everything = jax.tree.map(lambda part: lax.all_gather(part, axis), shard)  49.4 us
    all_gather x1, blocking collectives, per_device(): delta = lax.all_gather(local_delta, 'row', axis=0, tiled=True)  35.6 us
    reduce_scatter x1, waiting for transfers between devices, per_device(): lax.psum_scatter(grad_k.astype(jnp.bfloat16), 'col', scatter_dimension=0,...  31 us
    all_gather x1, blocking collectives, per_device(): lax.all_gather(keys, 'col', axis=0, tiled=True)  24.6 us
    all_gather x1, blocking collectives, per_device(): lax.all_gather(values, 'col', axis=0, tiled=True)  24.2 us
    dot_general x4, matrix products, tile_grads(): lax.dot_general(cot_head, value_all, (((1,), (1,)), ((), ())), preferred_...  16.3 us
    reduce_sum x1, other arithmetic, local_stats(): jnp.sum(jnp.where(causal, jnp.exp(scores - largest[:, None]), 0.0), axis=1)  10.3 us
  transfers between devices with their start and end apart: 5, of which 2 were waited for; matrix products, arithmetic and copies ran while one was open for 18% of the time, Pallas kernels for 0%

commit v1 on v0

v1 whole, which is shorter than its diff:
```python
import functools
import math

import jax
import jax.numpy as jnp
from jax import lax
from jax.experimental import pallas as pl
from jax.experimental.pallas import tpu as pltpu
from jax.sharding import PartitionSpec as P

MESH = pl.DeviceIdType.MESH
F32 = jnp.float32
BF16 = jnp.bfloat16
HIDDEN = -1e30

NQ = 8
NK = 16


def here():
    row = lax.axis_index("row")
    col = lax.axis_index("col")
    z = (row // 8) * 2 + col // 4
    return (row // 2) % 4, col % 4, z, row % 2


def device(x, y, z, core):
    return (((z // 2) * 4 + x) * 2 + core, (z % 2) * 4 + y)


def y_step(t):
    u = t // 2
    return u + (u // 2) * (5 - 2 * u)


def query_owner(t):
    x, y, z, core = here()
    return x, (y + 4 - y_step(t)) % 4, z, (core + t % 2) % 2


def query_reader(t):
    x, y, z, core = here()
    return x, (y + y_step(t)) % 4, z, (core + t % 2) % 2


def key_owner(j):
    x, y, z, core = here()
    return (x + 4 - j % 4) % 4, y, (z + 4 - j // 4) % 4, core


def key_reader(j):
    x, y, z, core = here()
    return (x + j % 4) % 4, y, (z + j // 4) % 4, core


def slot_of(place):
    row, col = device(*place)
    return row * 8 + col


def kernel(
    order,
    q_in,
    k_in,
    v_in,
    o_in,
    g_in,
    dq_out,
    dk_out,
    dv_out,
    qs,
    gs,
    own_o,
    delta,
    ks,
    vs,
    kt,
    scores,
    probs,
    dscores,
    u_mine,
    u_got,
    stat,
    stat_got,
    cmat,
    qc,
    gc,
    part,
    part_got,
    local_sem,
    q_send,
    q_recv,
    d_send,
    d_recv,
    k_send,
    k_recv,
    u_send,
    u_recv,
    s_send,
    s_recv,
    p_send,
    p_recv,
):
    dh = 128
    blk = 128
    heads = 4
    factor = 1.0 / math.sqrt(dh)
    scale2 = factor * math.log2(math.e)

    def remote(src, dst, send, recv, place):
        return pltpu.make_async_remote_copy(
            src_ref=src,
            dst_ref=dst,
            send_sem=send,
            recv_sem=recv,
            device_id=device(*place),
            device_id_type=MESH,
        )

    def q_copy(src_q, src_g, t, place):
        return (
            remote(src_q, qs.at[t], q_send.at[t, 0], q_recv.at[t, 0], place),
            remote(src_g, gs.at[t], q_send.at[t, 1], q_recv.at[t, 1], place),
        )

    def k_copy(j):
        rows = pl.ds(j * blk, blk)
        return (
            remote(k_in, ks.at[rows], k_send.at[j, 0], k_recv.at[j, 0], key_reader(j)),
            remote(v_in, vs.at[rows], k_send.at[j, 1], k_recv.at[j, 1], key_reader(j)),
        )

    def d_copy(t):
        return remote(delta.at[0], delta.at[t], d_send.at[t], d_recv.at[t], query_reader(t))

    def u_copy(t):
        return remote(u_mine.at[t], u_got.at[t], u_send.at[t], u_recv.at[t], query_owner(t))

    def s_copy(t):
        return remote(stat, stat_got.at[t], s_send.at[t], s_recv.at[t], query_owner(t))

    def p_copy(j):
        return remote(part.at[j], part_got.at[j], p_send.at[j], p_recv.at[j], key_owner(j))

    barrier = pltpu.get_barrier_semaphore()
    for t in range(1, NQ):
        pl.semaphore_signal(barrier, inc=1, device_id=device(*query_reader(t)), device_id_type=MESH)
    for j in range(1, NK):
        pl.semaphore_signal(barrier, inc=1, device_id=device(*key_reader(j)), device_id_type=MESH)
    locals_ = [
        pltpu.make_async_copy(o_in, own_o, local_sem.at[0]),
        pltpu.make_async_copy(g_in, gs.at[0], local_sem.at[1]),
        pltpu.make_async_copy(q_in, qs.at[0], local_sem.at[2]),
        pltpu.make_async_copy(k_in, ks.at[pl.ds(0, blk)], local_sem.at[3]),
        pltpu.make_async_copy(v_in, vs.at[pl.ds(0, blk)], local_sem.at[4]),
    ]
    for copy in locals_:
        copy.start()
    for copy in locals_:
        copy.wait()
    product = gs[0].astype(F32) * own_o[...].astype(F32)
    for h in range(heads):
        summed = jnp.sum(product[:, h * dh : (h + 1) * dh], axis=1, keepdims=True)
        wide = jnp.broadcast_to(summed, (blk, dh))
        delta[0, :, h * blk : (h + 1) * blk] = jnp.transpose(wide)[0:1, :]
    pl.semaphore_wait(barrier, NQ - 1 + NK - 1)

    for j in range(1, NK):
        for copy in k_copy(j):
            copy.start()
    for t in (1, 2, 4, 6):
        for copy in q_copy(q_in, g_in, t, query_reader(t)):
            copy.start()
    for t in range(1, NQ):
        d_copy(t).start()

    for j in range(1, NK):
        for copy in k_copy(j):
            copy.wait_recv()
    for j in range(NK):
        kt[:, j * blk : (j + 1) * blk] = jnp.transpose(
            ks[j * blk : (j + 1) * blk, :].astype(F32)
        ).astype(BF16)

    x, y, z, core = here()
    row_less_col = lax.broadcasted_iota(jnp.int32, (blk, 2 * blk), 0) - (
        lax.broadcasted_iota(jnp.int32, (blk, 2 * blk), 1) % blk
    )
    chunk = 256
    per_chunk = chunk // blk

    def step(t, carry):
        @pl.when(t > 0)
        def _():
            for copy in q_copy(q_in, g_in, t, query_reader(t)):
                copy.wait_recv()
            d_copy(t).wait_recv()

        @pl.when(jnp.logical_and(t > 1, t % 2 == 0))
        def _():
            for copy in q_copy(qs.at[t], gs.at[t], t + 1, (x, y, z, (core + 1) % 2)):
                copy.start()

        owner = query_owner(t)
        q_order = order[slot_of(owner)]
        group = owner[1] * 2 + owner[3]
        for pair in range(2):
            lanes = pl.ds(pl.multiple_of(t * 512 + pair * 256, 256), 256)
            own = slice(pair * 256, pair * 256 + 256)
            q2 = jnp.concatenate(
                [qs[t, :, (2 * pair + i) * dh : (2 * pair + i + 1) * dh] for i in range(2)], axis=0
            )
            g2 = jnp.concatenate(
                [gs[t, :, (2 * pair + i) * dh : (2 * pair + i + 1) * dh] for i in range(2)], axis=0
            )
            top8 = jnp.full((8, 256), HIDDEN, F32)
            penalty = []
            for first in range(0, NK, per_chunk):
                rows = slice(first * blk, (first + per_chunk) * blk)
                s = lax.dot_general(
                    ks[rows, :], q2, (((1,), (1,)), ((), ())), preferred_element_type=F32
                )
                for i in range(per_chunk):
                    j = first + i
                    tile = s[i * blk : (i + 1) * blk]
                    k_order = order[slot_of(key_owner(j))]
                    if j == 0:
                        tile = jnp.where(row_less_col <= blk * (q_order - k_order), tile, HIDDEN)
                        cost = jnp.float32(0.0)
                    else:
                        cost = jnp.where(k_order < q_order, 0.0, -HIDDEN).astype(F32)
                    penalty.append(cost)
                    scores[j * blk : (j + 1) * blk, :] = tile
                    largest = jnp.max(tile.reshape(blk // 8, 8, 256), axis=0)
                    top8 = jnp.maximum(top8, largest - cost)
            top = jnp.max(top8, axis=0, keepdims=True) * scale2
            total8 = jnp.zeros((8, 256), F32)
            du = jnp.zeros((dh, 256), F32)
            away = delta[t, :, own]
            for first in range(0, NK, per_chunk):
                rows = slice(first * blk, (first + per_chunk) * blk)
                dp = lax.dot_general(
                    vs[rows, :], g2, (((1,), (1,)), ((), ())), preferred_element_type=F32
                )
                pieces = []
                for i in range(per_chunk):
                    j = first + i
                    tile_rows = slice(j * blk, (j + 1) * blk)
                    p = jnp.exp2(scores[tile_rows, :] * scale2 - (top + penalty[j]))
                    total8 += jnp.sum(p.reshape(blk // 8, 8, 256), axis=0)
                    ds = (p * (dp[i * blk : (i + 1) * blk] - away)).astype(BF16)
                    probs[tile_rows, lanes] = p.astype(BF16)
                    dscores[tile_rows, lanes] = ds
                    pieces.append(ds)
                du += jnp.dot(
                    kt[:, rows], jnp.concatenate(pieces, axis=0), preferred_element_type=F32
                )
            u_mine[t, :, own] = du.astype(BF16)
            stat[0, pl.ds(group, 1), own] = top
            stat[1, pl.ds(group, 1), own] = jnp.sum(total8, axis=0, keepdims=True)

        @pl.when(t > 0)
        def _():
            u_copy(t).start()

        return carry

    lax.fori_loop(0, NQ, step, 0)

    for t in range(1, NQ):
        s_copy(t).start()
    for t in range(1, NQ):
        s_copy(t).wait_recv()
    tops = [stat[0]] + [stat_got[t, 0] for t in range(1, NQ)]
    best = functools.reduce(jnp.maximum, tops)
    total = stat[1] * jnp.exp2(tops[0] - best)
    for t in range(1, NQ):
        total += stat_got[t, 1] * jnp.exp2(tops[t] - best)
    log_total = best + jnp.log2(total)
    cmat[0] = jnp.exp2(stat[0] - log_total)
    for t in range(1, NQ):
        cmat[t] = jnp.exp2(stat_got[t, 0] - log_total)

    def line_of(matrix, place):
        line = lax.broadcasted_iota(jnp.int32, matrix.shape, 0)
        picked = jnp.where(line == place[1] * 2 + place[3], matrix, 0.0)
        return jnp.sum(picked, axis=0, keepdims=True)

    rows = []
    for t in range(NQ):
        line = line_of(cmat[0], query_owner(t))
        for h in range(heads):
            rows.append(line[:, h * blk : (h + 1) * blk])
    rows.append(jnp.zeros((blk - NQ * heads, blk), F32))
    columns = jnp.transpose(jnp.concatenate(rows, axis=0))
    for t in range(NQ):
        for h in range(heads):
            place = slice((t * heads + h) * blk, (t * heads + h + 1) * blk)
            c = columns[:, t * heads + h : t * heads + h + 1]
            qc[place, :] = (qs[t, :, h * dh : (h + 1) * dh].astype(F32) * c).astype(BF16)
            gc[place, :] = (gs[t, :, h * dh : (h + 1) * dh].astype(F32) * c).astype(BF16)

    def grads(i, carry):
        dz = 3 - i
        rows = pl.ds(pl.multiple_of(dz * 512, 512), 512)
        dv = jnp.dot(probs[rows, :], gc[...], preferred_element_type=F32)
        dk = jnp.dot(dscores[rows, :], qc[...], preferred_element_type=F32) * factor
        for n in range(4):
            j = dz * 4 + n
            part[j, 0] = dk[n * blk : (n + 1) * blk].astype(BF16)
            part[j, 1] = dv[n * blk : (n + 1) * blk].astype(BF16)

            @pl.when(j > 0)
            def _():
                p_copy(j).start()

        return carry

    lax.fori_loop(0, 4, grads, 0)

    for t in range(1, NQ):
        u_copy(t).wait_recv()
    weights = [line_of(cmat[t], (x, y, z, core)) * factor for t in range(NQ)]
    for h in range(heads):
        lanes = slice(h * blk, (h + 1) * blk)
        acc = weights[0][:, lanes] * u_mine[0, :, lanes].astype(F32)
        for t in range(1, NQ):
            acc += weights[t][:, lanes] * u_got[t, :, lanes].astype(F32)
        dq_out[:, h * dh : (h + 1) * dh] = jnp.transpose(acc).astype(BF16)

    for j in range(1, NK):
        p_copy(j).wait_recv()
    dk_sum = part[0, 0].astype(F32)
    dv_sum = part[0, 1].astype(F32)
    for j in range(1, NK):
        dk_sum += part_got[j, 0].astype(F32)
        dv_sum += part_got[j, 1].astype(F32)
    dk_out[...] = dk_sum.astype(BF16)
    dv_out[...] = dv_sum.astype(BF16)

    for j in range(1, NK):
        for copy in k_copy(j):
            copy.wait_send()
        p_copy(j).wait_send()
    for t in range(1, NQ):
        for copy in q_copy(q_in, g_in, t, query_reader(t)):
            copy.wait_send()
        d_copy(t).wait_send()
        u_copy(t).wait_send()
        s_copy(t).wait_send()


def per_device(queries, keys, values, outputs, grad_out, block_order):
    anywhere = pl.BlockSpec(memory_space=pl.ANY)
    whole = pl.BlockSpec(memory_space=pltpu.VMEM)
    dma = pltpu.SemaphoreType.DMA
    return pl.pallas_call(
        kernel,
        out_shape=(
            jax.ShapeDtypeStruct((128, 512), BF16),
            jax.ShapeDtypeStruct((128, 128), BF16),
            jax.ShapeDtypeStruct((128, 128), BF16),
        ),
        in_specs=[pl.BlockSpec(memory_space=pltpu.SMEM)] + [anywhere] * 5,
        out_specs=(whole, whole, whole),
        scratch_shapes=[
            pltpu.VMEM((NQ, 128, 512), BF16),
            pltpu.VMEM((NQ, 128, 512), BF16),
            pltpu.VMEM((128, 512), BF16),
            pltpu.VMEM((NQ, 1, 512), F32),
            pltpu.VMEM((2048, 128), BF16),
            pltpu.VMEM((2048, 128), BF16),
            pltpu.VMEM((128, 2048), BF16),
            pltpu.VMEM((2048, 256), F32),
            pltpu.VMEM((2048, 4096), BF16),
            pltpu.VMEM((2048, 4096), BF16),
            pltpu.VMEM((NQ, 128, 512), BF16),
            pltpu.VMEM((NQ, 128, 512), BF16),
            pltpu.VMEM((2, NQ, 512), F32),
            pltpu.VMEM((NQ, 2, NQ, 512), F32),
            pltpu.VMEM((NQ, NQ, 512), F32),
            pltpu.VMEM((4096, 128), BF16),
            pltpu.VMEM((4096, 128), BF16),
            pltpu.VMEM((NK, 2, 128, 128), BF16),
            pltpu.VMEM((NK, 2, 128, 128), BF16),
            dma((5,)),
            dma((NQ, 2)),
            dma((NQ, 2)),
            dma((NQ,)),
            dma((NQ,)),
            dma((NK, 2)),
            dma((NK, 2)),
            dma((NQ,)),
            dma((NQ,)),
            dma((NQ,)),
            dma((NQ,)),
            dma((NK,)),
            dma((NK,)),
        ],
        compiler_params=pltpu.CompilerParams(
            collective_id=0, has_side_effects=True, vmem_limit_bytes=60 * 1024 * 1024
        ),
        name="attention_backward",
    )(block_order, queries, keys, values, outputs, grad_out)


def solution(mesh):
    rows = P(("row", "col"), None)
    return jax.shard_map(
        per_device,
        mesh=mesh,
        in_specs=(rows, rows, rows, rows, rows, P()),
        out_specs=(rows, rows, rows),
        check_vma=False,
    )
```

time: 335 us -> 83.4 us (0.25)
  blocking collectives: 134 us -> 0 us
  waiting for transfers between devices: 110 us -> 0 us
  Pallas kernels: 0 us -> 79.6 us
  matrix products: 49.6 us -> 0 us
  other arithmetic: 14.2 us -> 0 us
  between operations: 14.2 us -> 0.65 us
  local copies, waits for them, and re-layouts: 11.1 us -> 2.96 us
    all_gather x5 -> x0, blocking collectives: 134 us -> none  [the longest x2 49.4 us: joined(): everything = jax.tree.map(lambda part: lax.all_gather(part, axis), shard)]
    pallas_call x0 -> x1, Pallas kernels: none -> 79.6 us  [per_device(): pl.pallas_call(kernel, out_shape=(jax.ShapeDtypeStruct((128, 512), BF16),...]
    unnamed x6 -> x0, waiting for transfers between devices: 79.1 us -> none
    dot_general x20 -> x0, matrix products: 49.6 us -> none  [the longest x4 16.3 us: tile_grads(): lax.dot_general(cot_head, value_all, (((1,), (1,)), ((), ())), preferred_...]
    reduce_scatter x2 -> x0, waiting for transfers between devices: 31 us -> none  [the longest x1 31 us: per_device(): lax.psum_scatter(grad_k.astype(jnp.bfloat16), 'col', scatter_dimension=0,...]
    reduce_sum x2 -> x0, other arithmetic: 10.5 us -> none  [the longest x1 10.3 us: local_stats(): jnp.sum(jnp.where(causal, jnp.exp(scores - largest[:, None]), 0.0), axis=1)]
    unnamed x41 -> x7, local copies, waits for them, and re-layouts: 7.69 us -> 2.96 us
  transfers between devices with their start and end apart: 5 -> 0, of which waited for: 2 -> 0; matrix products, arithmetic and copies ran while one was open for 18% -> 0% of each run, Pallas kernels for 0% -> 0%
where the time goes in v1:
time: 83.4 us; the launch traced here: 83.2 us
  Pallas kernels  79.6 us (95%)
  local copies, waits for them, and re-layouts  2.96 us (4%)
    pallas_call x1, Pallas kernels, per_device(): pl.pallas_call(kernel, out_shape=(jax.ShapeDtypeStruct((128, 512), BF16),...  79.6 us
    unnamed x7, local copies, waits for them, and re-layouts  2.96 us

profile of v1, /device:TPU:1, one launch (start us, length us, event | category | flops | bytes accessed | tf_op | source)
XLA Modules:
  0.0 83.2 jit_solution(9496309786279849667)
XLA Ops:
  0.6 79.6 %attention_backward.1 = (bf16[128,512]{1,0:T(8,128)(2,1)}, bf16[128,128]{1,0:T(8,128)(2,1)}, bf16[128,128]{1,0:T(8,128)(2,1)}) custom-call(s32[128]{0:T(128)} %order.1, bf16[128,512]{1,0:T(8,128)(2,1)} %q_in.1, bf16[128,128]{1,0:T(8,128)(2,1)} %k_in.1, bf16[128,128]{1,0:T(8,128)(2,1)} %v_in.1, bf16[128,512]{1,0:T(8,128)(2,1)} %o_in.1, bf16[128,512]{1,0:T(8,128)(2,1)} %g_in.1), custom_call_target="tpu_custom_call" | custom-call | tf_op jit(solution)/shard_map/attention_backward/pallas_call | solution.py:357
  80.2 0.0 copy-start.1
  80.2 1.6 %copy.12 = bf16[128,512]{1,0:T(8,128)(2,1)} copy(bf16[128,512]{1,0:T(8,128)(2,1)} %get-tuple-element.6) | data formatting | bytes 262144
  81.8 0.0 copy-done.1
  81.8 0.0 copy-start
  81.8 0.6 copy.13
  82.4 0.2 copy-done
  82.6 0.6 copy.14
Async XLA Ops:
  80.2 1.6 %copy-start.1 = (bf16[128,128]{1,0:T(8,128)(2,1)S(1)}, bf16[128,128]{1,0:T(8,128)(2,1)}, u32[]{:S(2)}) copy-start(bf16[128,128]{1,0:T(8,128)(2,1)} %get-tuple-element.7) | copy-start | bytes 98308
  81.8 0.8 copy-start

commit v2 on v1

--- a/solution.py
+++ b/solution.py
@@ -15,6 +15,12 @@
 
 NQ = 8
 NK = 16
+KEY_STEPS = (
+    ((0, 0), (1, 0), (3, 0), (0, 1), (0, 3), (1, 1), (3, 3), (1, 3))
+    + ((2, 2), (2, 1), (2, 3), (1, 2), (3, 2), (2, 0), (0, 2), (3, 1))
+)
+FAR_ORDER = (13, 14, 15, 9, 10, 11, 12, 8)
+HALF = 1024
 
 
 def here():
@@ -45,12 +51,23 @@
 
 def key_owner(j):
     x, y, z, core = here()
-    return (x + 4 - j % 4) % 4, y, (z + 4 - j // 4) % 4, core
+    dx, dz = KEY_STEPS[j]
+    return (x + 4 - dx) % 4, y, (z + 4 - dz) % 4, core
 
 
 def key_reader(j):
     x, y, z, core = here()
-    return (x + j % 4) % 4, y, (z + j // 4) % 4, core
+    dx, dz = KEY_STEPS[j]
+    return (x + dx) % 4, y, (z + dz) % 4, core
+
+
+def static_y(t):
+    return (0, 1, 3, 2)[t // 2]
+
+
+def seen_as(sender, t):
+    dy = (static_y(t) - static_y(sender)) % 4
+    return 2 * (0, 1, 3, 2)[dy] + (sender + t) % 2
 
 
 def slot_of(place):
@@ -78,11 +95,13 @@
     scores,
     probs,
     dscores,
+    u_sum,
     u_mine,
     u_got,
+    stat_first,
     stat,
     stat_got,
-    cmat,
+    columns,
     qc,
     gc,
     part,
@@ -136,8 +155,15 @@
     def u_copy(t):
         return remote(u_mine.at[t], u_got.at[t], u_send.at[t], u_recv.at[t], query_owner(t))
 
-    def s_copy(t):
-        return remote(stat, stat_got.at[t], s_send.at[t], s_recv.at[t], query_owner(t))
+    def s_copy(t, batch):
+        some = pl.ds(batch * 4, 4)
+        return remote(
+            stat.at[some],
+            stat_got.at[t, some],
+            s_send.at[t, batch],
+            s_recv.at[t, batch],
+            query_owner(t),
+        )
 
     def p_copy(j):
         return remote(part.at[j], part_got.at[j], p_send.at[j], p_recv.at[j], key_owner(j))
@@ -165,22 +191,31 @@
         delta[0, :, h * blk : (h + 1) * blk] = jnp.transpose(wide)[0:1, :]
     pl.semaphore_wait(barrier, NQ - 1 + NK - 1)
 
-    for j in range(1, NK):
-        for copy in k_copy(j):
-            copy.start()
-    for t in (1, 2, 4, 6):
+    def start_keys(slots):
+        for j in slots:
+            for copy in k_copy(j):
+                copy.start()
+
+    start_keys(range(1, 5))
+    for t in (1, 2, 4):
         for copy in q_copy(q_in, g_in, t, query_reader(t)):
             copy.start()
+    start_keys(range(5, 8))
     for t in range(1, NQ):
         d_copy(t).start()
-
-    for j in range(1, NK):
-        for copy in k_copy(j):
-            copy.wait_recv()
-    for j in range(NK):
-        kt[:, j * blk : (j + 1) * blk] = jnp.transpose(
-            ks[j * blk : (j + 1) * blk, :].astype(F32)
-        ).astype(BF16)
+    start_keys(FAR_ORDER)
+    for copy in q_copy(q_in, g_in, 6, query_reader(6)):
+        copy.start()
+
+    def take_keys(slots):
+        for j in slots:
+            if j > 0:
+                for copy in k_copy(j):
+                    copy.wait_recv()
+        for j in slots:
+            kt[:, j * blk : (j + 1) * blk] = jnp.transpose(
+                ks[j * blk : (j + 1) * blk, :].astype(F32)
+            ).astype(BF16)
 
     x, y, z, core = here()
     row_less_col = lax.broadcasted_iota(jnp.int32, (blk, 2 * blk), 0) - (
@@ -189,21 +224,9 @@
     chunk = 256
     per_chunk = chunk // blk
 
-    def step(t, carry):
-        @pl.when(t > 0)
-        def _():
-            for copy in q_copy(q_in, g_in, t, query_reader(t)):
-                copy.wait_recv()
-            d_copy(t).wait_recv()
-
-        @pl.when(jnp.logical_and(t > 1, t % 2 == 0))
-        def _():
-            for copy in q_copy(qs.at[t], gs.at[t], t + 1, (x, y, z, (core + 1) % 2)):
-                copy.start()
-
-        owner = query_owner(t)
-        q_order = order[slot_of(owner)]
-        group = owner[1] * 2 + owner[3]
+    def unit(t, half, with_u):
+        q_order = order[slot_of(query_owner(t))]
+        slots = range(half * 8, half * 8 + 8)
         for pair in range(2):
             lanes = pl.ds(pl.multiple_of(t * 512 + pair * 256, 256), 256)
             own = slice(pair * 256, pair * 256 + 256)
@@ -214,14 +237,15 @@
                 [gs[t, :, (2 * pair + i) * dh : (2 * pair + i + 1) * dh] for i in range(2)], axis=0
             )
             top8 = jnp.full((8, 256), HIDDEN, F32)
-            penalty = []
-            for first in range(0, NK, per_chunk):
+            penalty = {}
+            for first in slots[::per_chunk]:
                 rows = slice(first * blk, (first + per_chunk) * blk)
                 s = lax.dot_general(
                     ks[rows, :], q2, (((1,), (1,)), ((), ())), preferred_element_type=F32
                 )
                 for i in range(per_chunk):
                     j = first + i
+                    n = j - half * 8
                     tile = s[i * blk : (i + 1) * blk]
                     k_order = order[slot_of(key_owner(j))]
                     if j == 0:
@@ -229,15 +253,18 @@
                         cost = jnp.float32(0.0)
                     else:
                         cost = jnp.where(k_order < q_order, 0.0, -HIDDEN).astype(F32)
-                    penalty.append(cost)
-                    scores[j * blk : (j + 1) * blk, :] = tile
+                    penalty[j] = cost
+                    scores[n * blk : (n + 1) * blk, :] = tile
                     largest = jnp.max(tile.reshape(blk // 8, 8, 256), axis=0)
                     top8 = jnp.maximum(top8, largest - cost)
             top = jnp.max(top8, axis=0, keepdims=True) * scale2
+            if half == 1:
+                before = stat_first[t, 0:1, own]
+                top = jnp.maximum(top, before)
             total8 = jnp.zeros((8, 256), F32)
             du = jnp.zeros((dh, 256), F32)
             away = delta[t, :, own]
-            for first in range(0, NK, per_chunk):
+            for first in slots[::per_chunk]:
                 rows = slice(first * blk, (first + per_chunk) * blk)
                 dp = lax.dot_general(
                     vs[rows, :], g2, (((1,), (1,)), ((), ())), preferred_element_type=F32
@@ -245,19 +272,49 @@
                 pieces = []
                 for i in range(per_chunk):
                     j = first + i
+                    n = j - half * 8
                     tile_rows = slice(j * blk, (j + 1) * blk)
-                    p = jnp.exp2(scores[tile_rows, :] * scale2 - (top + penalty[j]))
+                    p = jnp.exp2(
+                        scores[n * blk : (n + 1) * blk, :] * scale2 - (top + penalty[j])
+                    )
                     total8 += jnp.sum(p.reshape(blk // 8, 8, 256), axis=0)
                     ds = (p * (dp[i * blk : (i + 1) * blk] - away)).astype(BF16)
                     probs[tile_rows, lanes] = p.astype(BF16)
                     dscores[tile_rows, lanes] = ds
                     pieces.append(ds)
-                du += jnp.dot(
-                    kt[:, rows], jnp.concatenate(pieces, axis=0), preferred_element_type=F32
-                )
-            u_mine[t, :, own] = du.astype(BF16)
-            stat[0, pl.ds(group, 1), own] = top
-            stat[1, pl.ds(group, 1), own] = jnp.sum(total8, axis=0, keepdims=True)
+                if with_u:
+                    du += jnp.dot(
+                        kt[:, rows], jnp.concatenate(pieces, axis=0), preferred_element_type=F32
+                    )
+            total = jnp.sum(total8, axis=0, keepdims=True)
+            if half == 0:
+                stat_first[t, 0:1, own] = top
+                stat_first[t, 1:2, own] = total
+                u_sum[t, :, own] = du
+            else:
+                shrink = jnp.exp2(before - top)
+                stat[t, 0:1, own] = top
+                stat[t, 1:2, own] = total + stat_first[t, 1:2, own] * shrink
+                if with_u:
+                    u_mine[t, :, own] = (du + u_sum[t, :, own] * shrink).astype(BF16)
+
+    def first_half(t, carry):
+        @pl.when(t > 0)
+        def _():
+            for copy in q_copy(q_in, g_in, t, query_reader(t)):
+                copy.wait_recv()
+            d_copy(t).wait_recv()
+
+        @pl.when(jnp.logical_and(t > 1, t % 2 == 0))
+        def _():
+            for copy in q_copy(qs.at[t], gs.at[t], t + 1, (x, y, z, (core + 1) % 2)):
+                copy.start()
+
+        unit(t, 0, True)
+        return carry
+
+    def second_half(t, carry):
+        unit(t, 1, True)
 
         @pl.when(t > 0)
         def _():
@@ -265,62 +322,86 @@
 
         return carry
 
-    lax.fori_loop(0, NQ, step, 0)
-
-    for t in range(1, NQ):
-        s_copy(t).start()
-    for t in range(1, NQ):
-        s_copy(t).wait_recv()
-    tops = [stat[0]] + [stat_got[t, 0] for t in range(1, NQ)]
-    best = functools.reduce(jnp.maximum, tops)
-    total = stat[1] * jnp.exp2(tops[0] - best)
-    for t in range(1, NQ):
-        total += stat_got[t, 1] * jnp.exp2(tops[t] - best)
-    log_total = best + jnp.log2(total)
-    cmat[0] = jnp.exp2(stat[0] - log_total)
-    for t in range(1, NQ):
-        cmat[t] = jnp.exp2(stat_got[t, 0] - log_total)
-
-    def line_of(matrix, place):
-        line = lax.broadcasted_iota(jnp.int32, matrix.shape, 0)
-        picked = jnp.where(line == place[1] * 2 + place[3], matrix, 0.0)
-        return jnp.sum(picked, axis=0, keepdims=True)
-
-    rows = []
-    for t in range(NQ):
-        line = line_of(cmat[0], query_owner(t))
-        for h in range(heads):
-            rows.append(line[:, h * blk : (h + 1) * blk])
-    rows.append(jnp.zeros((blk - NQ * heads, blk), F32))
-    columns = jnp.transpose(jnp.concatenate(rows, axis=0))
-    for t in range(NQ):
-        for h in range(heads):
-            place = slice((t * heads + h) * blk, (t * heads + h + 1) * blk)
-            c = columns[:, t * heads + h : t * heads + h + 1]
-            qc[place, :] = (qs[t, :, h * dh : (h + 1) * dh].astype(F32) * c).astype(BF16)
-            gc[place, :] = (gs[t, :, h * dh : (h + 1) * dh].astype(F32) * c).astype(BF16)
-
-    def grads(i, carry):
-        dz = 3 - i
-        rows = pl.ds(pl.multiple_of(dz * 512, 512), 512)
+    def second_half_late(t, carry):
+        unit(t, 1, False)
+        return carry
+
+    def late_u(t, carry):
+        lanes = pl.ds(pl.multiple_of(t * 512, 512), 512)
+        du = jnp.dot(kt[:, HALF:], dscores[HALF:, lanes], preferred_element_type=F32)
+        shrink = jnp.exp2(stat_first[t, 0:1, :] - stat[t, 0:1, :])
+        u_mine[t] = (du + u_sum[t] * shrink).astype(BF16)
+        u_copy(t).start()
+        return carry
+
+    take_keys(range(8))
+    lax.fori_loop(0, NQ, first_half, 0)
+    take_keys(range(8, NK))
+    lax.fori_loop(0, 4, second_half, 0)
+    for t in range(1, NQ):
+        s_copy(t, 0).start()
+    lax.fori_loop(4, NQ, second_half_late, 0)
+    for t in range(1, NQ):
+        s_copy(t, 1).start()
+    lax.fori_loop(4, NQ, late_u, 0)
+
+    for t in range(1, NQ):
+        for batch in range(2):
+            s_copy(t, batch).wait_recv()
+    found = {n: [] for n in range(NQ)}
+    for sender in range(NQ):
+        for t in range(NQ):
+            from_ = stat[t] if sender == 0 else stat_got[sender, t]
+            found[seen_as(sender, t)].append((from_[0:1], from_[1:2]))
+    log_totals = []
+    for n in range(NQ):
+        best = functools.reduce(jnp.maximum, [top for top, _ in found[n]])
+        total = sum(part_total * jnp.exp2(top - best) for top, part_total in found[n])
+        log_totals.append(best + jnp.log2(total))
+    lines = []
+    for source in (stat_first, stat):
+        for t in range(NQ):
+            line = jnp.exp2(source[t, 0:1, :] - log_totals[t])
+            for h in range(heads):
+                lines.append(line[:, h * blk : (h + 1) * blk])
+    lines.append(jnp.zeros((blk - 2 * NQ * heads, blk), F32))
+    columns[...] = jnp.transpose(jnp.concatenate(lines, axis=0))
+    weights = []
+    for sender in range(NQ):
+        t = [n for n in range(NQ) if seen_as(sender, n) == 0][0]
+        top = stat[t, 0:1, :] if sender == 0 else stat_got[sender, t, 0:1, :]
+        weights.append(jnp.exp2(top - log_totals[0]) * factor)
+
+    def scaled_rows(half):
+        for t in range(NQ):
+            for h in range(heads):
+                n = t * heads + h
+                c = columns[:, half * NQ * heads + n : half * NQ * heads + n + 1]
+                place = slice(n * blk, (n + 1) * blk)
+                lanes = slice(h * dh, (h + 1) * dh)
+                qc[place, :] = (qs[t, :, lanes].astype(F32) * c).astype(BF16)
+                gc[place, :] = (gs[t, :, lanes].astype(F32) * c).astype(BF16)
+
+    def key_grads(first):
+        rows = slice(first * blk, (first + 4) * blk)
         dv = jnp.dot(probs[rows, :], gc[...], preferred_element_type=F32)
         dk = jnp.dot(dscores[rows, :], qc[...], preferred_element_type=F32) * factor
         for n in range(4):
-            j = dz * 4 + n
+            j = first + n
             part[j, 0] = dk[n * blk : (n + 1) * blk].astype(BF16)
             part[j, 1] = dv[n * blk : (n + 1) * blk].astype(BF16)
-
-            @pl.when(j > 0)
-            def _():
+            if j > 0:
                 p_copy(j).start()
 
-        return carry
-
-    lax.fori_loop(0, 4, grads, 0)
+    scaled_rows(1)
+    key_grads(8)
+    key_grads(12)
+    scaled_rows(0)
+    key_grads(4)
+    key_grads(0)
 
     for t in range(1, NQ):
         u_copy(t).wait_recv()
-    weights = [line_of(cmat[t], (x, y, z, core)) * factor for t in range(NQ)]
     for h in range(heads):
         lanes = slice(h * blk, (h + 1) * blk)
         acc = weights[0][:, lanes] * u_mine[0, :, lanes].astype(F32)
@@ -347,7 +428,8 @@
             copy.wait_send()
         d_copy(t).wait_send()
         u_copy(t).wait_send()
-        s_copy(t).wait_send()
+        for batch in range(2):
+            s_copy(t, batch).wait_send()
 
 
 def per_device(queries, keys, values, outputs, grad_out, block_order):
@@ -371,14 +453,16 @@
             pltpu.VMEM((2048, 128), BF16),
             pltpu.VMEM((2048, 128), BF16),
             pltpu.VMEM((128, 2048), BF16),
-            pltpu.VMEM((2048, 256), F32),
+            pltpu.VMEM((HALF, 256), F32),
             pltpu.VMEM((2048, 4096), BF16),
             pltpu.VMEM((2048, 4096), BF16),
+            pltpu.VMEM((NQ, 128, 512), F32),
             pltpu.VMEM((NQ, 128, 512), BF16),
             pltpu.VMEM((NQ, 128, 512), BF16),
-            pltpu.VMEM((2, NQ, 512), F32),
-            pltpu.VMEM((NQ, 2, NQ, 512), F32),
-            pltpu.VMEM((NQ, NQ, 512), F32),
+            pltpu.VMEM((NQ, 2, 512), F32),
+            pltpu.VMEM((NQ, 2, 512), F32),
+            pltpu.VMEM((NQ, NQ, 2, 512), F32),
+            pltpu.VMEM((128, 128), F32),
             pltpu.VMEM((4096, 128), BF16),
             pltpu.VMEM((4096, 128), BF16),
             pltpu.VMEM((NK, 2, 128, 128), BF16),
@@ -392,8 +476,8 @@
             dma((NK, 2)),
             dma((NQ,)),
             dma((NQ,)),
-            dma((NQ,)),
-            dma((NQ,)),
+            dma((NQ, 2)),
+            dma((NQ, 2)),
             dma((NK,)),
             dma((NK,)),
         ],

time: 83.4 us -> 69.9 us (0.84)
  Pallas kernels: 79.6 us -> 66 us
    pallas_call x1, Pallas kernels: 79.6 us -> 66 us  [per_device(): pl.pallas_call(kernel, out_shape=(jax.ShapeDtypeStruct((128, 512), BF16),...]
where the time goes in v2:
time: 69.9 us; the launch traced here: 69.6 us
  Pallas kernels  66 us (94%)
  local copies, waits for them, and re-layouts  2.96 us (4%)
    pallas_call x1, Pallas kernels, per_device(): pl.pallas_call(kernel, out_shape=(jax.ShapeDtypeStruct((128, 512), BF16),...  66 us
    unnamed x7, local copies, waits for them, and re-layouts  2.96 us

profile of v2, /device:TPU:1, one launch (start us, length us, event | category | flops | bytes accessed | tf_op | source)
XLA Modules:
  0.0 69.6 jit_solution(9504817915568325041)
XLA Ops:
  0.6 66.0 %attention_backward.1 = (bf16[128,512]{1,0:T(8,128)(2,1)}, bf16[128,128]{1,0:T(8,128)(2,1)}, bf16[128,128]{1,0:T(8,128)(2,1)}) custom-call(s32[128]{0:T(128)} %order.1, bf16[128,512]{1,0:T(8,128)(2,1)} %q_in.1, bf16[128,128]{1,0:T(8,128)(2,1)} %k_in.1, bf16[128,128]{1,0:T(8,128)(2,1)} %v_in.1, bf16[128,512]{1,0:T(8,128)(2,1)} %o_in.1, bf16[128,512]{1,0:T(8,128)(2,1)} %g_in.1), custom_call_target="tpu_custom_call" | custom-call | tf_op jit(solution)/shard_map/attention_backward/pallas_call | solution.py:439
  66.7 0.0 copy-start.1
  66.7 1.6 %copy.12 = bf16[128,512]{1,0:T(8,128)(2,1)} copy(bf16[128,512]{1,0:T(8,128)(2,1)} %get-tuple-element.6) | data formatting | bytes 262144
  68.3 0.0 copy-done.1
  68.3 0.0 copy-start
  68.3 0.6 copy.13
  68.9 0.2 copy-done
  69.0 0.6 copy.14
Async XLA Ops:
  66.7 1.6 %copy-start.1 = (bf16[128,128]{1,0:T(8,128)(2,1)S(1)}, bf16[128,128]{1,0:T(8,128)(2,1)}, u32[]{:S(2)}) copy-start(bf16[128,128]{1,0:T(8,128)(2,1)} %get-tuple-element.7) | copy-start | bytes 98308
  68.3 0.8 %copy-start = (bf16[128,128]{1,0:T(8,128)(2,1)S(1)}, bf16[128,128]{1,0:T(8,128)(2,1)}, u32[]{:S(2)}) copy-start(bf16[128,128]{1,0:T(8,128)(2,1)} %get-tuple-element.8) | copy-start | bytes 98308

commit v3 on v2

--- a/solution.py
+++ b/solution.py
@@ -17,9 +17,11 @@
 NK = 16
 KEY_STEPS = (
     ((0, 0), (1, 0), (3, 0), (0, 1), (0, 3), (1, 1), (3, 3), (1, 3))
-    + ((2, 2), (2, 1), (2, 3), (1, 2), (3, 2), (2, 0), (0, 2), (3, 1))
+    + ((2, 1), (2, 3), (1, 2), (3, 2), (2, 0), (0, 2), (2, 2), (3, 1))
 )
-FAR_ORDER = (13, 14, 15, 9, 10, 11, 12, 8)
+NEAR = (1, 2, 3, 4, 5, 6, 7, 15)
+FAR = (12, 13, 8, 9, 10, 11)
+CORNER = 14
 HALF = 1024
 
 
@@ -59,6 +61,23 @@
     x, y, z, core = here()
     dx, dz = KEY_STEPS[j]
     return (x + dx) % 4, y, (z + dz) % 4, core
+
+
+def key_step(j, part):
+    size = 1 if part == 0 else 3
+    dx, dz = KEY_STEPS[j]
+    return (size, 0) if dx == 2 else (0, size)
+
+
+def halfway(j, part):
+    step = key_step(j, part)
+    dx, dz = KEY_STEPS[j]
+    return KEY_STEPS.index(((dx - step[0]) % 4, (dz - step[1]) % 4))
+
+
+def neighbour(step, sign):
+    x, y, z, core = here()
+    return (x + 4 + sign * step[0]) % 4, y, (z + 4 + sign * step[1]) % 4, core
 
 
 def static_y(t):
@@ -106,6 +125,7 @@
     gc,
     part,
     part_got,
+    relayed,
     local_sem,
     q_send,
     q_recv,
@@ -119,6 +139,8 @@
     s_recv,
     p_send,
     p_recv,
+    r_send,
+    r_recv,
 ):
     dh = 128
     blk = 128
@@ -149,6 +171,25 @@
             remote(v_in, vs.at[rows], k_send.at[j, 1], k_recv.at[j, 1], key_reader(j)),
         )
 
+    def relay_keys(j, part):
+        ref = (ks, vs)[part]
+        return remote(
+            ref.at[pl.ds(halfway(j, part) * blk, blk)],
+            ref.at[pl.ds(j * blk, blk)],
+            k_send.at[j, part],
+            k_recv.at[j, part],
+            neighbour(key_step(j, part), 1),
+        )
+
+    def relay_grads(j, part_):
+        return remote(
+            part.at[j, part_],
+            relayed.at[j - 8, part_],
+            r_send.at[j - 8, part_],
+            r_recv.at[j - 8, part_],
+            neighbour(key_step(j, part_), -1),
+        )
+
     def d_copy(t):
         return remote(delta.at[0], delta.at[t], d_send.at[t], d_recv.at[t], query_reader(t))
 
@@ -171,7 +212,7 @@
     barrier = pltpu.get_barrier_semaphore()
     for t in range(1, NQ):
         pl.semaphore_signal(barrier, inc=1, device_id=device(*query_reader(t)), device_id_type=MESH)
-    for j in range(1, NK):
+    for j in NEAR + (CORNER,):
         pl.semaphore_signal(barrier, inc=1, device_id=device(*key_reader(j)), device_id_type=MESH)
     locals_ = [
         pltpu.make_async_copy(o_in, own_o, local_sem.at[0]),
@@ -189,29 +230,24 @@
         summed = jnp.sum(product[:, h * dh : (h + 1) * dh], axis=1, keepdims=True)
         wide = jnp.broadcast_to(summed, (blk, dh))
         delta[0, :, h * blk : (h + 1) * blk] = jnp.transpose(wide)[0:1, :]
-    pl.semaphore_wait(barrier, NQ - 1 + NK - 1)
+    pl.semaphore_wait(barrier, NQ - 1 + len(NEAR) + 1)
 
     def start_keys(slots):
         for j in slots:
             for copy in k_copy(j):
                 copy.start()
 
-    start_keys(range(1, 5))
+    start_keys(NEAR)
     for t in (1, 2, 4):
         for copy in q_copy(q_in, g_in, t, query_reader(t)):
             copy.start()
-    start_keys(range(5, 8))
     for t in range(1, NQ):
         d_copy(t).start()
-    start_keys(FAR_ORDER)
+    start_keys((CORNER,))
     for copy in q_copy(q_in, g_in, 6, query_reader(6)):
         copy.start()
 
-    def take_keys(slots):
-        for j in slots:
-            if j > 0:
-                for copy in k_copy(j):
-                    copy.wait_recv()
+    def turn_keys(slots):
         for j in slots:
             kt[:, j * blk : (j + 1) * blk] = jnp.transpose(
                 ks[j * blk : (j + 1) * blk, :].astype(F32)
@@ -221,72 +257,79 @@
     row_less_col = lax.broadcasted_iota(jnp.int32, (blk, 2 * blk), 0) - (
         lax.broadcasted_iota(jnp.int32, (blk, 2 * blk), 1) % blk
     )
-    chunk = 256
+    chunk = 512
     per_chunk = chunk // blk
 
     def unit(t, half, with_u):
         q_order = order[slot_of(query_owner(t))]
         slots = range(half * 8, half * 8 + 8)
+        penalty = {}
+        for j in slots[1 - half :]:
+            k_order = order[slot_of(key_owner(j))]
+            penalty[j] = jnp.where(k_order < q_order, 0.0, -HIDDEN).astype(F32)
+
+        def two_heads(ref, pair):
+            return jnp.concatenate(
+                [ref[t, :, (2 * pair + i) * dh : (2 * pair + i + 1) * dh] for i in range(2)], axis=0
+            )
+
+        def score_part(pair, q2, first, top8):
+            rows = slice(first * blk, (first + per_chunk) * blk)
+            s = lax.dot_general(
+                ks[rows, :], q2, (((1,), (1,)), ((), ())), preferred_element_type=F32
+            )
+            for i in range(per_chunk):
+                j = first + i
+                n = j - half * 8
+                tile = s[i * blk : (i + 1) * blk]
+                if j == 0:
+                    k_order = order[slot_of(key_owner(0))]
+                    tile = jnp.where(row_less_col <= blk * (q_order - k_order), tile, HIDDEN)
+                scores[pair, n * blk : (n + 1) * blk, :] = tile
+                largest = jnp.max(tile.reshape(blk // 8, 8, 256), axis=0)
+                top8 = jnp.maximum(top8, largest - penalty[j] if j > 0 else largest)
+            return top8
+
+        def grad_part(pair, g2, first, top, away, total8):
+            lanes = pl.ds(pl.multiple_of(t * 512 + pair * 256, 256), 256)
+            rows = slice(first * blk, (first + per_chunk) * blk)
+            dp = lax.dot_general(
+                vs[rows, :], g2, (((1,), (1,)), ((), ())), preferred_element_type=F32
+            )
+            for i in range(per_chunk):
+                j = first + i
+                n = j - half * 8
+                tile_rows = slice(j * blk, (j + 1) * blk)
+                shift = top + penalty[j] if j > 0 else top
+                p = jnp.exp2(scores[pair, n * blk : (n + 1) * blk, :] * scale2 - shift)
+                total8 += jnp.sum(p.reshape(blk // 8, 8, 256), axis=0)
+                ds = p * (dp[i * blk : (i + 1) * blk] - away)
+                probs[tile_rows, lanes] = p.astype(BF16)
+                dscores[tile_rows, lanes] = ds.astype(BF16)
+            return total8
+
+        queries = [two_heads(qs, pair) for pair in range(2)]
+        top8 = [jnp.full((8, 256), HIDDEN, F32) for pair in range(2)]
+        for first in slots[::per_chunk]:
+            top8[0] = score_part(0, queries[0], first, top8[0])
         for pair in range(2):
-            lanes = pl.ds(pl.multiple_of(t * 512 + pair * 256, 256), 256)
             own = slice(pair * 256, pair * 256 + 256)
-            q2 = jnp.concatenate(
-                [qs[t, :, (2 * pair + i) * dh : (2 * pair + i + 1) * dh] for i in range(2)], axis=0
-            )
-            g2 = jnp.concatenate(
-                [gs[t, :, (2 * pair + i) * dh : (2 * pair + i + 1) * dh] for i in range(2)], axis=0
-            )
-            top8 = jnp.full((8, 256), HIDDEN, F32)
-            penalty = {}
-            for first in slots[::per_chunk]:
-                rows = slice(first * blk, (first + per_chunk) * blk)
-                s = lax.dot_general(
-                    ks[rows, :], q2, (((1,), (1,)), ((), ())), preferred_element_type=F32
-                )
-                for i in range(per_chunk):
-                    j = first + i
-                    n = j - half * 8
-                    tile = s[i * blk : (i + 1) * blk]
-                    k_order = order[slot_of(key_owner(j))]
-                    if j == 0:
-                        tile = jnp.where(row_less_col <= blk * (q_order - k_order), tile, HIDDEN)
-                        cost = jnp.float32(0.0)
-                    else:
-                        cost = jnp.where(k_order < q_order, 0.0, -HIDDEN).astype(F32)
-                    penalty[j] = cost
-                    scores[n * blk : (n + 1) * blk, :] = tile
-                    largest = jnp.max(tile.reshape(blk // 8, 8, 256), axis=0)
-                    top8 = jnp.maximum(top8, largest - cost)
-            top = jnp.max(top8, axis=0, keepdims=True) * scale2
+            top = jnp.max(top8[pair], axis=0, keepdims=True) * scale2
             if half == 1:
                 before = stat_first[t, 0:1, own]
                 top = jnp.maximum(top, before)
             total8 = jnp.zeros((8, 256), F32)
-            du = jnp.zeros((dh, 256), F32)
+            g2 = two_heads(gs, pair)
             away = delta[t, :, own]
             for first in slots[::per_chunk]:
-                rows = slice(first * blk, (first + per_chunk) * blk)
-                dp = lax.dot_general(
-                    vs[rows, :], g2, (((1,), (1,)), ((), ())), preferred_element_type=F32
-                )
-                pieces = []
-                for i in range(per_chunk):
-                    j = first + i
-                    n = j - half * 8
-                    tile_rows = slice(j * blk, (j + 1) * blk)
-                    p = jnp.exp2(
-                        scores[n * blk : (n + 1) * blk, :] * scale2 - (top + penalty[j])
-                    )
-                    total8 += jnp.sum(p.reshape(blk // 8, 8, 256), axis=0)
-                    ds = (p * (dp[i * blk : (i + 1) * blk] - away)).astype(BF16)
-                    probs[tile_rows, lanes] = p.astype(BF16)
-                    dscores[tile_rows, lanes] = ds
-                    pieces.append(ds)
-                if with_u:
-                    du += jnp.dot(
-                        kt[:, rows], jnp.concatenate(pieces, axis=0), preferred_element_type=F32
-                    )
+                if pair == 0:
+                    top8[1] = score_part(1, queries[1], first, top8[1])
+                total8 = grad_part(pair, g2, first, top, away, total8)
             total = jnp.sum(total8, axis=0, keepdims=True)
+            if with_u:
+                lanes = pl.ds(pl.multiple_of(t * 512 + pair * 256, 256), 256)
+                keys_ = slice(half * HALF, (half + 1) * HALF)
+                du = jnp.dot(kt[:, keys_], dscores[keys_, lanes], preferred_element_type=F32)
             if half == 0:
                 stat_first[t, 0:1, own] = top
                 stat_first[t, 1:2, own] = total
@@ -334,9 +377,18 @@
         u_copy(t).start()
         return carry
 
-    take_keys(range(8))
+    for j in NEAR:
+        for part_, copy in enumerate(k_copy(j)):
+            copy.wait_recv()
+            for far in FAR:
+                if halfway(far, part_) == j:
+                    relay_keys(far, part_).start()
+    turn_keys(range(8))
     lax.fori_loop(0, NQ, first_half, 0)
-    take_keys(range(8, NK))
+    for j in FAR + (CORNER,):
+        for copy in k_copy(j):
+            copy.wait_recv()
+    turn_keys(range(8, NK))
     lax.fori_loop(0, 4, second_half, 0)
     for t in range(1, NQ):
         s_copy(t, 0).start()
@@ -390,15 +442,34 @@
             j = first + n
             part[j, 0] = dk[n * blk : (n + 1) * blk].astype(BF16)
             part[j, 1] = dv[n * blk : (n + 1) * blk].astype(BF16)
-            if j > 0:
-                p_copy(j).start()
+
+    def send_near(slots):
+        for j in slots:
+            for part_ in range(2):
+                total = part[j, part_].astype(F32)
+                extra = [far for far in FAR if halfway(far, part_) == j]
+                for far in extra:
+                    relay_grads(far, part_).wait_recv()
+                    total += relayed[far - 8, part_].astype(F32)
+                if extra:
+                    part[j, part_] = total.astype(BF16)
+            p_copy(j).start()
 
     scaled_rows(1)
     key_grads(8)
+    for j in (8, 9, 10, 11):
+        for part_ in range(2):
+            relay_grads(j, part_).start()
     key_grads(12)
+    for j in (12, 13):
+        for part_ in range(2):
+            relay_grads(j, part_).start()
+    p_copy(CORNER).start()
     scaled_rows(0)
     key_grads(4)
+    send_near((5, 6, 7, 15))
     key_grads(0)
+    send_near((1, 2, 3, 4))
 
     for t in range(1, NQ):
         u_copy(t).wait_recv()
@@ -409,20 +480,23 @@
             acc += weights[t][:, lanes] * u_got[t, :, lanes].astype(F32)
         dq_out[:, h * dh : (h + 1) * dh] = jnp.transpose(acc).astype(BF16)
 
-    for j in range(1, NK):
-        p_copy(j).wait_recv()
     dk_sum = part[0, 0].astype(F32)
     dv_sum = part[0, 1].astype(F32)
-    for j in range(1, NK):
+    for j in (CORNER, 5, 6, 7, 15, 1, 2, 3, 4):
+        p_copy(j).wait_recv()
         dk_sum += part_got[j, 0].astype(F32)
         dv_sum += part_got[j, 1].astype(F32)
     dk_out[...] = dk_sum.astype(BF16)
     dv_out[...] = dv_sum.astype(BF16)
 
-    for j in range(1, NK):
+    for j in NEAR + (CORNER,):
         for copy in k_copy(j):
             copy.wait_send()
         p_copy(j).wait_send()
+    for j in FAR:
+        for part_ in range(2):
+            relay_keys(j, part_).wait_send()
+            relay_grads(j, part_).wait_send()
     for t in range(1, NQ):
         for copy in q_copy(q_in, g_in, t, query_reader(t)):
             copy.wait_send()
@@ -453,7 +527,7 @@
             pltpu.VMEM((2048, 128), BF16),
             pltpu.VMEM((2048, 128), BF16),
             pltpu.VMEM((128, 2048), BF16),
-            pltpu.VMEM((HALF, 256), F32),
+            pltpu.VMEM((2, HALF, 256), F32),
             pltpu.VMEM((2048, 4096), BF16),
             pltpu.VMEM((2048, 4096), BF16),
             pltpu.VMEM((NQ, 128, 512), F32),
@@ -467,6 +541,7 @@
             pltpu.VMEM((4096, 128), BF16),
             pltpu.VMEM((NK, 2, 128, 128), BF16),
             pltpu.VMEM((NK, 2, 128, 128), BF16),
+            pltpu.VMEM((6, 2, 128, 128), BF16),
             dma((5,)),
             dma((NQ, 2)),
             dma((NQ, 2)),
@@ -480,6 +555,8 @@
             dma((NQ, 2)),
             dma((NK,)),
             dma((NK,)),
+            dma((6, 2)),
+            dma((6, 2)),
         ],
         compiler_params=pltpu.CompilerParams(
             collective_id=0, has_side_effects=True, vmem_limit_bytes=60 * 1024 * 1024

time: 69.9 us -> 66.3 us (0.948)
  the two profiles are of different devices: /device:TPU:1 before, /device:TPU:9 now
where the time goes in v3:
time: 66.3 us; the launch traced here: 66.1 us
  Pallas kernels  62.5 us (94%)
  local copies, waits for them, and re-layouts  2.96 us (4%)
    pallas_call x1, Pallas kernels, per_device(): pl.pallas_call(kernel, out_shape=(jax.ShapeDtypeStruct((128, 512), BF16),...  62.5 us
    unnamed x7, local copies, waits for them, and re-layouts  2.96 us

profile of v3, /device:TPU:9, one launch (start us, length us, event | category | flops | bytes accessed | tf_op | source)
XLA Modules:
  0.0 66.1 jit_solution(9324895112651942089)
XLA Ops:
  0.6 62.5 %attention_backward.1 = (bf16[128,512]{1,0:T(8,128)(2,1)}, bf16[128,128]{1,0:T(8,128)(2,1)}, bf16[128,128]{1,0:T(8,128)(2,1)}) custom-call(s32[128]{0:T(128)} %order.1, bf16[128,512]{1,0:T(8,128)(2,1)} %q_in.1, bf16[128,128]{1,0:T(8,128)(2,1)} %k_in.1, bf16[128,128]{1,0:T(8,128)(2,1)} %v_in.1, bf16[128,512]{1,0:T(8,128)(2,1)} %o_in.1, bf16[128,512]{1,0:T(8,128)(2,1)} %g_in.1), custom_call_target="tpu_custom_call" | custom-call | tf_op jit(solution)/shard_map/attention_backward/pallas_call | solution.py:513
  63.1 0.0 copy-start.1
  63.1 1.6 %copy.12 = bf16[128,512]{1,0:T(8,128)(2,1)} copy(bf16[128,512]{1,0:T(8,128)(2,1)} %get-tuple-element.6) | data formatting | bytes 262144
  64.7 0.0 copy-done.1
  64.7 0.0 copy-start
  64.7 0.6 copy.13
  65.3 0.2 copy-done
  65.5 0.6 copy.14
Async XLA Ops:
  63.1 1.6 %copy-start.1 = (bf16[128,128]{1,0:T(8,128)(2,1)S(1)}, bf16[128,128]{1,0:T(8,128)(2,1)}, u32[]{:S(2)}) copy-start(bf16[128,128]{1,0:T(8,128)(2,1)} %get-tuple-element.7) | copy-start | bytes 98308
  64.7 0.8 %copy-start = (bf16[128,128]{1,0:T(8,128)(2,1)S(1)}, bf16[128,128]{1,0:T(8,128)(2,1)}, u32[]{:S(2)}) copy-start(bf16[128,128]{1,0:T(8,128)(2,1)} %get-tuple-element.8) | copy-start | bytes 98308

commit v4 on v3

--- a/solution.py
+++ b/solution.py
@@ -23,6 +23,7 @@
 FAR = (12, 13, 8, 9, 10, 11)
 CORNER = 14
 HALF = 1024
+STAT_BATCHES = ((6, 2), (0, 2), (2, 4))
 
 
 def here():
@@ -197,7 +198,7 @@
         return remote(u_mine.at[t], u_got.at[t], u_send.at[t], u_recv.at[t], query_owner(t))
 
     def s_copy(t, batch):
-        some = pl.ds(batch * 4, 4)
+        some = pl.ds(*STAT_BATCHES[batch])
         return remote(
             stat.at[some],
             stat_got.at[t, some],
@@ -356,7 +357,8 @@
         unit(t, 0, True)
         return carry
 
-    def second_half(t, carry):
+    def second_half(i, carry):
+        t = (i + 6) % NQ
         unit(t, 1, True)
 
         @pl.when(t > 0)
@@ -392,13 +394,14 @@
     lax.fori_loop(0, 4, second_half, 0)
     for t in range(1, NQ):
         s_copy(t, 0).start()
-    lax.fori_loop(4, NQ, second_half_late, 0)
-    for t in range(1, NQ):
         s_copy(t, 1).start()
-    lax.fori_loop(4, NQ, late_u, 0)
-
-    for t in range(1, NQ):
-        for batch in range(2):
+    lax.fori_loop(2, 6, second_half_late, 0)
+    for t in range(1, NQ):
+        s_copy(t, 2).start()
+    lax.fori_loop(2, 6, late_u, 0)
+
+    for t in range(1, NQ):
+        for batch in range(len(STAT_BATCHES)):
             s_copy(t, batch).wait_recv()
     found = {n: [] for n in range(NQ)}
     for sender in range(NQ):
@@ -434,11 +437,11 @@
                 qc[place, :] = (qs[t, :, lanes].astype(F32) * c).astype(BF16)
                 gc[place, :] = (gs[t, :, lanes].astype(F32) * c).astype(BF16)
 
-    def key_grads(first):
-        rows = slice(first * blk, (first + 4) * blk)
+    def key_grads(first, count):
+        rows = slice(first * blk, (first + count) * blk)
         dv = jnp.dot(probs[rows, :], gc[...], preferred_element_type=F32)
         dk = jnp.dot(dscores[rows, :], qc[...], preferred_element_type=F32) * factor
-        for n in range(4):
+        for n in range(count):
             j = first + n
             part[j, 0] = dk[n * blk : (n + 1) * blk].astype(BF16)
             part[j, 1] = dv[n * blk : (n + 1) * blk].astype(BF16)
@@ -456,20 +459,21 @@
             p_copy(j).start()
 
     scaled_rows(1)
-    key_grads(8)
+    key_grads(8, 4)
     for j in (8, 9, 10, 11):
         for part_ in range(2):
             relay_grads(j, part_).start()
-    key_grads(12)
+    key_grads(12, 4)
     for j in (12, 13):
         for part_ in range(2):
             relay_grads(j, part_).start()
     p_copy(CORNER).start()
     scaled_rows(0)
-    key_grads(4)
-    send_near((5, 6, 7, 15))
-    key_grads(0)
-    send_near((1, 2, 3, 4))
+    key_grads(4, 4)
+    send_near((5, 6, 7, 15, 4))
+    key_grads(1, 3)
+    send_near((1, 2, 3))
+    key_grads(0, 1)
 
     for t in range(1, NQ):
         u_copy(t).wait_recv()
@@ -502,7 +506,7 @@
             copy.wait_send()
         d_copy(t).wait_send()
         u_copy(t).wait_send()
-        for batch in range(2):
+        for batch in range(len(STAT_BATCHES)):
             s_copy(t, batch).wait_send()
 
 
@@ -551,8 +555,8 @@
             dma((NK, 2)),
             dma((NQ,)),
             dma((NQ,)),
-            dma((NQ, 2)),
-            dma((NQ, 2)),
+            dma((NQ, len(STAT_BATCHES))),
+            dma((NQ, len(STAT_BATCHES))),
             dma((NK,)),
             dma((NK,)),
             dma((6, 2)),

time: 66.3 us -> 62.1 us (0.937)
  the two profiles are of different devices: /device:TPU:9 before, /device:TPU:1 now
where the time goes in v4:
time: 62.1 us; the launch traced here: 61.9 us
  Pallas kernels  58.2 us (94%)
  local copies, waits for them, and re-layouts  2.96 us (5%)
  between operations  0.65 us (1%)
    pallas_call x1, Pallas kernels, per_device(): pl.pallas_call(kernel, out_shape=(jax.ShapeDtypeStruct((128, 512), BF16),...  58.2 us
    unnamed x7, local copies, waits for them, and re-layouts  2.96 us

profile of v4, /device:TPU:1, one launch (start us, length us, event | category | flops | bytes accessed | tf_op | source)
XLA Modules:
  0.0 61.9 jit_solution(13807052313388208231)
XLA Ops:
  0.6 58.2 %attention_backward.1 = (bf16[128,512]{1,0:T(8,128)(2,1)}, bf16[128,128]{1,0:T(8,128)(2,1)}, bf16[128,128]{1,0:T(8,128)(2,1)}) custom-call(s32[128]{0:T(128)} %order.1, bf16[128,512]{1,0:T(8,128)(2,1)} %q_in.1, bf16[128,128]{1,0:T(8,128)(2,1)} %k_in.1, bf16[128,128]{1,0:T(8,128)(2,1)} %v_in.1, bf16[128,512]{1,0:T(8,128)(2,1)} %o_in.1, bf16[128,512]{1,0:T(8,128)(2,1)} %g_in.1), custom_call_target="tpu_custom_call" | custom-call | tf_op jit(solution)/shard_map/attention_backward/pallas_call | solution.py:517
  58.9 0.0 copy-start.1
  58.9 1.6 %copy.12 = bf16[128,512]{1,0:T(8,128)(2,1)} copy(bf16[128,512]{1,0:T(8,128)(2,1)} %get-tuple-element.6) | data formatting | bytes 262144
  60.5 0.0 copy-done.1
  60.5 0.0 copy-start
  60.5 0.6 copy.13
  61.1 0.2 copy-done
  61.2 0.6 copy.14
Async XLA Ops:
  58.9 1.6 %copy-start.1 = (bf16[128,128]{1,0:T(8,128)(2,1)S(1)}, bf16[128,128]{1,0:T(8,128)(2,1)}, u32[]{:S(2)}) copy-start(bf16[128,128]{1,0:T(8,128)(2,1)} %get-tuple-element.7) | copy-start | bytes 98308
  60.5 0.8 %copy-start = (bf16[128,128]{1,0:T(8,128)(2,1)S(1)}, bf16[128,128]{1,0:T(8,128)(2,1)}, u32[]{:S(2)}) copy-start(bf16[128,128]{1,0:T(8,128)(2,1)} %get-tuple-element.8) | copy-start | bytes 98308

commit v5 on v4

--- a/solution.py
+++ b/solution.py
@@ -234,9 +234,10 @@
     pl.semaphore_wait(barrier, NQ - 1 + len(NEAR) + 1)
 
     def start_keys(slots):
-        for j in slots:
-            for copy in k_copy(j):
-                copy.start()
+        copies = [k_copy(j) for j in slots]
+        for part_ in range(2):
+            for pair in copies:
+                pair[part_].start()
 
     start_keys(NEAR)
     for t in (1, 2, 4):
@@ -244,7 +245,6 @@
             copy.start()
     for t in range(1, NQ):
         d_copy(t).start()
-    start_keys((CORNER,))
     for copy in q_copy(q_in, g_in, 6, query_reader(6)):
         copy.start()
 
@@ -385,6 +385,7 @@
             for far in FAR:
                 if halfway(far, part_) == j:
                     relay_keys(far, part_).start()
+    start_keys((CORNER,))
     turn_keys(range(8))
     lax.fori_loop(0, NQ, first_half, 0)
     for j in FAR + (CORNER,):

time: 62.1 us -> 61.1 us (0.984)
  Pallas kernels: 58.2 us -> 57.3 us
    pallas_call x1, Pallas kernels: 58.2 us -> 57.3 us  [per_device(): pl.pallas_call(kernel, out_shape=(jax.ShapeDtypeStruct((128, 512), BF16),...]
where the time goes in v5:
time: 61.1 us; the launch traced here: 60.9 us
  Pallas kernels  57.3 us (94%)
  local copies, waits for them, and re-layouts  2.96 us (5%)
  between operations  0.65 us (1%)
    pallas_call x1, Pallas kernels, per_device(): pl.pallas_call(kernel, out_shape=(jax.ShapeDtypeStruct((128, 512), BF16),...  57.3 us
    unnamed x7, local copies, waits for them, and re-layouts  2.96 us

profile of v5, /device:TPU:1, one launch (start us, length us, event | category | flops | bytes accessed | tf_op | source)
XLA Modules:
  0.0 60.9 jit_solution(11853664113899098432)
XLA Ops:
  0.6 57.3 %attention_backward.1 = (bf16[128,512]{1,0:T(8,128)(2,1)}, bf16[128,128]{1,0:T(8,128)(2,1)}, bf16[128,128]{1,0:T(8,128)(2,1)}) custom-call(s32[128]{0:T(128)} %order.1, bf16[128,512]{1,0:T(8,128)(2,1)} %q_in.1, bf16[128,128]{1,0:T(8,128)(2,1)} %k_in.1, bf16[128,128]{1,0:T(8,128)(2,1)} %v_in.1, bf16[128,512]{1,0:T(8,128)(2,1)} %o_in.1, bf16[128,512]{1,0:T(8,128)(2,1)} %g_in.1), custom_call_target="tpu_custom_call" | custom-call | tf_op jit(solution)/shard_map/attention_backward/pallas_call | solution.py:518
  57.9 0.0 copy-start.1
  58.0 1.6 %copy.12 = bf16[128,512]{1,0:T(8,128)(2,1)} copy(bf16[128,512]{1,0:T(8,128)(2,1)} %get-tuple-element.6) | data formatting | bytes 262144
  59.5 0.0 copy-done.1
  59.5 0.0 copy-start
  59.5 0.6 %copy.13 = bf16[128,128]{1,0:T(8,128)(2,1)} copy(bf16[128,128]{1,0:T(8,128)(2,1)S(1)} %copy-done.1) | data formatting | bytes 65536
  60.2 0.2 copy-done
  60.3 0.6 %copy.14 = bf16[128,128]{1,0:T(8,128)(2,1)} copy(bf16[128,128]{1,0:T(8,128)(2,1)S(1)} %copy-done) | data formatting | bytes 65536
Async XLA Ops:
  57.9 1.6 %copy-start.1 = (bf16[128,128]{1,0:T(8,128)(2,1)S(1)}, bf16[128,128]{1,0:T(8,128)(2,1)}, u32[]{:S(2)}) copy-start(bf16[128,128]{1,0:T(8,128)(2,1)} %get-tuple-element.7) | copy-start | bytes 98308
  59.5 0.8 %copy-start = (bf16[128,128]{1,0:T(8,128)(2,1)S(1)}, bf16[128,128]{1,0:T(8,128)(2,1)}, u32[]{:S(2)}) copy-start(bf16[128,128]{1,0:T(8,128)(2,1)} %get-tuple-element.8) | copy-start | bytes 98308
